TPU v7x, 256 devices: a whole 4x4x8 slice. The times are simulated.
256 devices in a mesh: seq: 32 (over z, y), ch: 8 (over x, core).
Axes of the slice: x: 4, y: 4, z: 8, core: 2. Of those that a mesh axis runs over, the one named last changes fastest.
Arguments:
- signal: float32 [32768, 1536], P('seq', 'ch'), may hold values from -6 to 6
- cotangent: float32 [32768, 1536], P('seq', 'ch'), may hold values from -6 to 6
- kernel_q: float32 [3, 1536], P(None, 'ch'), may hold values from -3 to 3
- kernel_k: float32 [3, 1536], P(None, 'ch'), may hold values from -3 to 3
- block_first: float32 [32, 1024, 1024], P('seq'), may hold values from -0.1875 to 0.1875
- block_second: float32 [32, 1024, 1024], P('seq'), may hold values from -0.1875 to 0.1875
- mix_self: float32 [5, 32, 1536], P(None, 'seq', 'ch'), may hold values from 0.5 to 1
- mix_partner: float32 [5, 32, 1536], P(None, 'seq', 'ch'), may hold values from -1 to 1
Outputs:
- output: float32 [32768, 1536], P('seq', 'ch')
- grad_signal: float32 [32768, 1536], P('seq', 'ch')
- grad_kernel_q: float32 [3, 1536], P(None, 'ch')
- grad_kernel_k: float32 [3, 1536], P(None, 'ch')
- grad_block_first: float32 [32, 1024, 1024], P('seq', 'ch')
- grad_block_second: float32 [32, 1024, 1024], P('seq', 'ch')
- grad_mix_self: float32 [5, 32, 1536], P(None, 'seq', 'ch')
- grad_mix_partner: float32 [5, 32, 1536], P(None, 'seq', 'ch')
All inputs are finite; a program needn't handle non-finite values.
Results may differ from a plain program's by a relative error of at most 0.00015.
Values sent between devices are 32-bit elements; how exact they have to be, the bound alone decides.
No kernel may reach another device: no remote copies, remote signals or barrier semaphores. Data moves between devices by JAX's collectives and lax.ppermute only.
A program may use at most 128 MiB of HBM per device.

v0:
```python
import math

import jax
import jax.numpy as jnp
from jax import lax
from jax.sharding import PartitionSpec as P

D = 1536


exact_mode = lax.Precision.HIGHEST


def with_halo(block, sides, width):
    for axis, dim in sides:
        count = lax.axis_size(axis)
        forward = [(i, i + 1) for i in range(count - 1)]
        backward = [(target, source) for source, target in forward]
        low = lax.ppermute(
            lax.slice_in_dim(block, block.shape[dim] - width, None, axis=dim), axis, forward
        )
        high = lax.ppermute(lax.slice_in_dim(block, 0, width, axis=dim), axis, backward)
        block = jnp.concatenate([low, block, high], axis=dim)
    return block


def partner_2(shard, axis, bit):
    return lax.ppermute(shard, axis, [(i, i ^ 1 << bit) for i in range(lax.axis_size(axis))])


def matmul(left, right):
    return jnp.dot(left, right, precision=exact_mode, preferred_element_type=jnp.float32)


def left_transposed(left, right):
    return lax.dot_general(
        left,
        right,
        (((0,), (0,)), ((), ())),
        precision=exact_mode,
        preferred_element_type=jnp.float32,
    )


def right_transposed(left, right):
    return lax.dot_general(
        left,
        right,
        (((1,), (1,)), ((), ())),
        precision=exact_mode,
        preferred_element_type=jnp.float32,
    )


def apply_taps(padded, taps_table):
    return taps_table[0] * padded[:-2] + taps_table[1] * padded[1:-1] + taps_table[2] * padded[2:]


def tap_sums(grad_rows, padded):
    return jnp.stack(
        [
            jnp.sum(grad_rows * padded[:-2], axis=0),
            jnp.sum(grad_rows * padded[1:-1], axis=0),
            jnp.sum(grad_rows * padded[2:], axis=0),
        ]
    )


def local(signal, cotangent, kernel_q, kernel_k, block_first, block_second, mix_self, mix_partner):
    height, breadth = signal.shape
    sections = mix_self.shape[0]
    blocks = lax.axis_size("seq")
    padded = with_halo(signal, (("seq", 0),), 1)
    query_conv = apply_taps(padded, kernel_q)
    key_conv = apply_taps(padded, kernel_k)
    gated_in = key_conv * signal
    first_out = matmul(block_first[0], gated_in)
    own_list = []
    partner_list = []
    current = first_out
    for section_bit in range(sections):
        partner = partner_2(current, "seq", section_bit)
        own_list.append(current)
        partner_list.append(partner)
        current = mix_self[section_bit] * current + mix_partner[section_bit] * partner
    mixed_out = matmul(block_second[0], current)
    output = query_conv * mixed_out
    grad_mixed = cotangent * query_conv
    grad_query = cotangent * mixed_out
    grad_last = left_transposed(block_second[0], grad_mixed)
    grad_second = right_transposed(grad_mixed, current)
    self_grads = [None] * sections
    partner_grads = [None] * sections
    grad_level = grad_last
    for section_bit in reversed(range(sections)):
        self_grads[section_bit] = jnp.sum(grad_level * own_list[section_bit], axis=0)
        partner_grads[section_bit] = jnp.sum(grad_level * partner_list[section_bit], axis=0)
        returned = partner_2(mix_partner[section_bit] * grad_level, "seq", section_bit)
        grad_level = mix_self[section_bit] * grad_level + returned
    grad_self_rows = jnp.stack(self_grads)[:, None, :]
    grad_partner_rows = jnp.stack(partner_grads)[:, None, :]
    grad_gated = left_transposed(block_first[0], grad_level)
    grad_block = right_transposed(grad_level, gated_in)
    width_scale = 1.0 / math.sqrt(D)
    summed_first, summed_second = (
        lax.psum_scatter(grad_block[None], "ch", scatter_dimension=1, tiled=True),
        lax.psum_scatter(grad_second[None], "ch", scatter_dimension=1, tiled=True),
    )
    grad_key = grad_gated * signal
    grad_signal = grad_gated * key_conv
    stacked = jnp.stack([grad_query, grad_key])
    edge_pad = with_halo(stacked, (("seq", 1),), 1)
    grad_signal = (
        grad_signal
        + kernel_q[0] * edge_pad[0, 2:]
        + kernel_q[1] * edge_pad[0, 1:-1]
        + kernel_q[2] * edge_pad[0, :-2]
    )
    grad_signal = (
        grad_signal
        + kernel_k[0] * edge_pad[1, 2:]
        + kernel_k[1] * edge_pad[1, 1:-1]
        + kernel_k[2] * edge_pad[1, :-2]
    )
    kernel_terms = jnp.stack([tap_sums(grad_query, padded), tap_sums(grad_key, padded)])
    kernel_total = lax.psum(kernel_terms, "seq")
    tok_scale = 1.0 / math.sqrt(height * blocks)
    row_scale = 1.0 / math.sqrt(height)
    return (
        output,
        grad_signal,
        kernel_total[0] * tok_scale,
        kernel_total[1] * tok_scale,
        summed_first * width_scale,
        summed_second * width_scale,
        grad_self_rows * row_scale,
        grad_partner_rows * row_scale,
    )


def solution(mesh):
    return jax.shard_map(
        local,
        mesh=mesh,
        in_specs=(
            P("seq", "ch"),
            P("seq", "ch"),
            P(None, "ch"),
            P(None, "ch"),
            P("seq", None, None),
            P("seq", None, None),
            P(None, "seq", "ch"),
            P(None, "seq", "ch"),
        ),
        out_specs=(
            P("seq", "ch"),
            P("seq", "ch"),
            P(None, "ch"),
            P(None, "ch"),
            P("seq", "ch", None),
            P("seq", "ch", None),
            P(None, "seq", "ch"),
            P(None, "seq", "ch"),
        ),
        check_vma=False,
    )
```

profile of v0, /device:TPU:6, one launch (start us, length us, event | category | flops | bytes accessed | tf_op | source)
XLA Modules:
  0.0 408.9 jit_solution(15662643185103263824)
XLA Ops:
  7.2 0.0 reduce-scatter.5.cloned.1.call-start
  7.2 1.0 fusion.40
  8.3 3.5 collective-permute-start
  11.8 1.3 collective-permute-start.1
  13.1 0.8 fusion.44
  13.9 0.1 collective-permute-done
  14.0 4.3 %collective-permute-done.1 = f32[1,192]{0,1:T(8,128)S(1)} collective-permute-done((f32[1,192]{0,1:T(8,128)S(1)}, f32[1,192]{0,1:T(8,128)S(1)}, u32[]{:S(2)}, u32[]{:S(2)}) %collective-permute-start.1) | collective-permute-done | bytes 800 | tf_op jit(solution)/shard_map/ppermute | solution.py:22
  18.3 8.0 %fusion.8 = f32[1024,192]{0,1:T(8,128)S(1)} fusion(f32[1,1024,1024]{2,1,0:T(8,128)} %param.12, f32[1024,192]{0,1:T(8,128)} %param.8, f32[192]{0:T(256)S(1)} %bitcast.129, f32[1,192]{0,1:T(8,128)S(1)} %collective-permute-done, f32[1,192]{0,1:T(8,128)S(1)} %collective-permute-done.1, f32[192]{0:T(256)S(1)} %bitcast.132, f32[192]{0:T(256)S(1)} %bitcast.126), kind=kOutput, calls=%fused_computation.10 | convolution fusion | flops 2417491968 | bytes 5771008 | tf_op jit(solution)/shard_map/dot_general | solution.py:32
  26.3 1.7 collective-permute-start.2
  28.0 16.2 %collective-permute-done.2 = f32[1024,192]{0,1:T(8,128)S(1)} collective-permute-done((f32[1024,192]{0,1:T(8,128)S(1)}, f32[1024,192]{0,1:T(8,128)S(1)}, u32[]{:S(2)}, u32[]{:S(2)}) %collective-permute-start.2) | collective-permute-done | bytes 786464 | tf_op jit(solution)/shard_map/ppermute | solution.py:28
  44.2 0.2 multiply_add_fusion.9
  44.4 5.0 %collective-permute-start.3 = (f32[1024,192]{0,1:T(8,128)S(1)}, f32[1024,192]{0,1:T(8,128)S(1)}, u32[]{:S(2)}, u32[]{:S(2)}) collective-permute-start(f32[1024,192]{0,1:T(8,128)S(1)} %multiply_add_fusion.9), channel_id=1, source_target_pairs={{0,16},{8,24},{16,0},{24,8},{32,48},{40,56},{48,32},{56,40},{64,80... | collective-permute-start | bytes 2359304 | tf_op jit(solution)/shard_map/ppermute | solution.py:28
  49.4 16.3 %collective-permute-done.3 = f32[1024,192]{0,1:T(8,128)S(1)} collective-permute-done((f32[1024,192]{0,1:T(8,128)S(1)}, f32[1024,192]{0,1:T(8,128)S(1)}, u32[]{:S(2)}, u32[]{:S(2)}) %collective-permute-start.3) | collective-permute-done | bytes 786464 | tf_op jit(solution)/shard_map/ppermute | solution.py:28
  65.6 0.2 multiply_add_fusion.8
  65.8 2.0 collective-permute-start.4
  67.9 3.2 broadcast_multiply_fusion
  71.1 5.5 %collective-permute-start.7 = (f32[1024,192]{0,1:T(8,128)S(1)}, f32[1024,192]{0,1:T(8,128)S(1)}, u32[]{:S(2)}, u32[]{:S(2)}) collective-permute-start(f32[1024,192]{0,1:T(8,128)S(1)} %get-tuple-element.57), channel_id=1, source_target_pairs={{0,128},{8,136},{16,144},{24,152},{32,160},{40,168},{48,176},{56,1... | collective-permute-start | bytes 2359304 | tf_op jit(solution)/shard_map/ppermute | solution.py:28
  76.5 10.4 %collective-permute-done.4 = f32[1024,192]{0,1:T(8,128)S(1)} collective-permute-done((f32[1024,192]{0,1:T(8,128)S(1)}, f32[1024,192]{0,1:T(8,128)S(1)}, u32[]{:S(2)}, u32[]{:S(2)}) %collective-permute-start.4) | collective-permute-done | bytes 786464 | tf_op jit(solution)/shard_map/ppermute | solution.py:28
  86.9 0.2 multiply_add_fusion.7
  87.1 21.5 %collective-permute-start.5 = (f32[1024,192]{0,1:T(8,128)S(1)}, f32[1024,192]{0,1:T(8,128)S(1)}, u32[]{:S(2)}, u32[]{:S(2)}) collective-permute-start(f32[1024,192]{0,1:T(8,128)S(1)} %multiply_add_fusion.7), channel_id=1, source_target_pairs={{0,64},{8,72},{16,80},{24,88},{32,96},{40,104},{48,112},{56,120},{... | collective-permute-start | bytes 2359304 | tf_op jit(solution)/shard_map/ppermute | solution.py:28
  108.6 2.8 collective-permute-done.7
  111.3 42.3 %collective-permute-done.5 = f32[1024,192]{0,1:T(8,128)S(1)} collective-permute-done((f32[1024,192]{0,1:T(8,128)S(1)}, f32[1024,192]{0,1:T(8,128)S(1)}, u32[]{:S(2)}, u32[]{:S(2)}) %collective-permute-start.5) | collective-permute-done | bytes 786464 | tf_op jit(solution)/shard_map/ppermute | solution.py:28
  153.6 1.3 multiply_reduce_fusion.1
  154.9 1.6 collective-permute-start.6
  156.5 34.5 %collective-permute-done.6 = f32[1024,192]{0,1:T(8,128)} collective-permute-done((f32[1024,192]{0,1:T(8,128)S(1)}, f32[1024,192]{0,1:T(8,128)}, u32[]{:S(2)}, u32[]{:S(2)}) %collective-permute-start.6) | collective-permute-done | bytes 786464 | tf_op jit(solution)/shard_map/ppermute | solution.py:28
  191.0 7.3 %convolution_bitcast_fusion = f32[1,1024,1024]{2,1,0:T(8,128)} fusion(f32[1024,192]{0,1:T(8,128)S(1)} %copy-done.5, f32[1024,192]{0,1:T(8,128)} %collective-permute-done.6, f32[1024,192]{0,1:T(8,128)S(1)} %get-tuple-element.36, f32[192]{0:T(256)S(1)} %bitcast.142, f32[192]{0:T(256)S(1)} %bitcast.139, f32[1024,192]{0,1:T(8,128)S(1)} %copy-done, ...), kind=kOutput, calls=%fused_computation.8 | convolution fusion | flops 2418081792 | bytes 7345408 | tf_op jit(solution)/shard_map/dot_general | solution.py:46
  198.3 0.0 reduce-scatter.5.cloned.1.call-update
  198.3 0.0 reduce-scatter.3.cloned.1.call-start
  198.4 0.0 copy-start.12
  198.4 1.3 broadcast_multiply_fusion.1
  199.7 0.1 collective-permute-start.8
  199.8 35.7 %collective-permute-done.8 = f32[1024,192]{0,1:T(8,128)S(1)} collective-permute-done((f32[1024,192]{0,1:T(8,128)S(1)}, f32[1024,192]{0,1:T(8,128)S(1)}, u32[]{:S(2)}, u32[]{:S(2)}) %collective-permute-start.8) | collective-permute-done | bytes 786464 | tf_op jit(solution)/shard_map/ppermute | solution.py:28
  235.5 2.0 multiply_reduce_fusion.2
  237.5 0.1 broadcast_multiply_fusion.2
  237.7 0.1 collective-permute-start.9
  237.8 17.1 %collective-permute-done.9 = f32[1024,192]{0,1:T(8,128)S(1)} collective-permute-done((f32[1024,192]{0,1:T(8,128)S(1)}, f32[1024,192]{0,1:T(8,128)S(1)}, u32[]{:S(2)}, u32[]{:S(2)}) %collective-permute-start.9) | collective-permute-done | bytes 786464 | tf_op jit(solution)/shard_map/ppermute | solution.py:28
  254.9 0.4 multiply_reduce_fusion.3
  255.3 0.1 broadcast_multiply_fusion.3
  255.4 0.3 collective-permute-start.10
  255.7 17.5 %collective-permute-done.10 = f32[1024,192]{0,1:T(8,128)S(1)} collective-permute-done((f32[1024,192]{0,1:T(8,128)S(1)}, f32[1024,192]{0,1:T(8,128)S(1)}, u32[]{:S(2)}, u32[]{:S(2)}) %collective-permute-start.10) | collective-permute-done | bytes 786464 | tf_op jit(solution)/shard_map/ppermute | solution.py:28
  273.2 0.3 multiply_reduce_fusion.4
  273.5 0.1 broadcast_multiply_fusion.4
  273.7 0.1 collective-permute-start.11
  273.8 15.3 %collective-permute-done.11 = f32[1024,192]{0,1:T(8,128)S(1)} collective-permute-done((f32[1024,192]{0,1:T(8,128)S(1)}, f32[1024,192]{0,1:T(8,128)S(1)}, u32[]{:S(2)}, u32[]{:S(2)}) %collective-permute-start.11) | collective-permute-done | bytes 786464 | tf_op jit(solution)/shard_map/ppermute | solution.py:28
  289.0 0.9 copy-done.14
  289.9 6.3 %convolution_bitcast_fusion.1 = f32[1,1024,1024]{2,1,0:T(8,128)} fusion(f32[1024,192]{0,1:T(8,128)S(1)} %collective-permute-done.11, f32[1024,192]{0,1:T(8,128)S(1)} %get-tuple-element.30, f32[192]{0:T(256)S(1)} %bitcast.136, f32[1024,192]{0,1:T(8,128)S(1)} %copy-done, f32[192]{0:T(256)S(1)} %bitcast.130, f32[1,192]{0,1:T(8,128)S(1)} %collective-permute-done, ...), kind=kOutput, calls=%fused_computation.9 | convolution fusion | flops 2417885184 | bytes 6558208 | tf_op jit(solution)/shard_map/dot_general | solution.py:46
  296.2 0.0 reduce-scatter.3.cloned.1.call-update
  296.2 0.0 copy-start.2
  296.2 0.0 copy-start.6
  296.2 1.5 multiply_reduce_fusion
  297.9 0.6 broadcast_multiply_fusion.7
  298.5 5.2 %fusion.11 = f32[1024,192]{0,1:T(8,128)S(1)} fusion(f32[1,1024,1024]{2,1,0:T(8,128)} %param.12, f32[1024,192]{0,1:T(8,128)} %copy-done.14, f32[1024,192]{0,1:T(8,128)S(1)} %get-tuple-element.30, f32[192]{0:T(256)S(1)} %bitcast.137), kind=kOutput, calls=%fused_computation.11 | convolution fusion | flops 2416312320 | bytes 6554368 | tf_op jit(solution)/shard_map/dot_general | solution.py:36
  303.7 0.0 copy-start.8
  303.7 7.0 %multiply_reduce_fusion.12 = (f32[192]{0:T(256)S(1)}, f32[192]{0:T(256)S(1)}, f32[192]{0:T(256)S(1)}, f32[192]{0:T(256)S(1)}, f32[192]{0:T(256)S(1)}, /*index=5*...) fusion(f32[1024,192]{0,1:T(8,128)S(1)} %copy-done, ...), kind=kOutput, calls=%fused_computation.46 | convolution fusion | flops 2420833280 | bytes 10495744 | tf_op jit(solution)/shard_map/dot_general | solution.py:32
  310.7 0.1 pad_maximum_fusion.7
  310.8 1.3 collective-permute-start.12
  312.1 4.6 %collective-permute-start.13 = (f32[2,1,192]{1,2,0:T(8,128)S(1)}, f32[2,1,192]{1,2,0:T(8,128)S(1)}, u32[]{:S(2)}, u32[]{:S(2)}) collective-permute-start(f32[2,1,192]{1,2,0:T(8,128)S(1)} %get-tuple-element.35), channel_id=1, source_target_pairs={{0,8},{8,16},{16,24},{24,32},{32,40},{40,48},{48,56},{56,64},{64,7... | collective-permute-start | bytes 4616 | tf_op jit(solution)/shard_map/ppermute | solution.py:19
  316.7 77.2 %psum.7 = f32[2,3,192]{2,1,0:T(4,128)S(1)} all-reduce(f32[2,3,192]{2,1,0:T(4,128)S(1)} %pad_maximum_fusion.8), channel_id=1, replica_groups=mesh['seq'=32,'ch'=8] {'seq'}, use_global_device_ids=true, to_apply=%region_6.0 | all-reduce | flops 1152 | bytes 9216 | tf_op jit(solution)/shard_map/psum | solution.py:126
  393.9 0.6 fusion.35
  394.5 0.0 collective-permute-done.12
  394.5 0.0 collective-permute-done.13
  394.5 3.8 fusion.22
  398.3 1.9 broadcast_multiply_fusion.5
  400.2 1.9 broadcast_multiply_fusion.6
  (48 shorter events, 0.2 us)
Async XLA Ops:
  7.2 20.8 %copy-start.15 = (f32[5,1,192]{2,1,0:T(1,128)S(1)}, f32[5,1,192]{2,1,0:T(1,128)}, u32[]{:S(2)}) copy-start(f32[5,1,192]{2,1,0:T(1,128)} %param.14) | copy-start | bytes 11524
  7.2 20.8 %copy-start.16 = (f32[5,1,192]{2,1,0:T(1,128)S(1)}, f32[5,1,192]{2,1,0:T(1,128)}, u32[]{:S(2)}) copy-start(f32[5,1,192]{2,1,0:T(1,128)} %param.15) | copy-start | bytes 11524
  7.2 391.1 %reduce-scatter.5.cloned.1.call-start = ((), (), s32[]{:S(2)}) async-start(), calls=%async_computation.3 | async-start | bytes 4718592 | tf_op jit(solution)/shard_map/reduce_scatter | solution.py:107
  8.3 5.7 %collective-permute-start = (f32[1,192]{0,1:T(8,128)S(1)}, f32[1,192]{0,1:T(8,128)S(1)}, u32[]{:S(2)}, u32[]{:S(2)}) collective-permute-start(f32[1,192]{0,1:T(8,128)S(1)} %get-tuple-element.38), channel_id=1, source_target_pairs={{0,8},{8,16},{16,24},{24,32},{32,40},{40,48},{48,56},{56,64},{64,7... | collective-permute-start | bytes 2312 | tf_op jit(solution)/shard_map/ppermute | solution.py:19
  11.8 6.5 %collective-permute-start.1 = (f32[1,192]{0,1:T(8,128)S(1)}, f32[1,192]{0,1:T(8,128)S(1)}, u32[]{:S(2)}, u32[]{:S(2)}) collective-permute-start(f32[1,192]{0,1:T(8,128)S(1)} %get-tuple-element.37), channel_id=1, source_target_pairs={{8,0},{16,8},{24,16},{32,24},{40,32},{48,40},{56,48},{64,56},{72,6... | collective-permute-start | bytes 2312 | tf_op jit(solution)/shard_map/ppermute | solution.py:22
  18.3 49.5 %copy-start.17 = (f32[3,192]{1,0:T(4,128)S(1)}, f32[3,192]{1,0:T(4,128)}, u32[]{:S(2)}) copy-start(f32[3,192]{1,0:T(4,128)} %param.10) | copy-start | bytes 6916
  18.3 49.6 %copy-start = (f32[1024,192]{0,1:T(8,128)S(1)}, f32[1024,192]{0,1:T(8,128)}, u32[]{:S(2)}) copy-start(f32[1024,192]{0,1:T(8,128)} %param.8) | copy-start | bytes 2359300
  18.3 49.6 %copy-start.1 = (f32[1,1024,1024]{2,1,0:T(8,128)S(1)}, f32[1,1024,1024]{2,1,0:T(8,128)}, u32[]{:S(2)}) copy-start(f32[1,1024,1024]{2,1,0:T(8,128)} %param.13) | copy-start | bytes 12582916
  18.3 49.6 %copy-start.5 = (f32[1024,192]{0,1:T(8,128)S(1)}, f32[1024,192]{0,1:T(8,128)}, u32[]{:S(2)}) copy-start(f32[1024,192]{0,1:T(8,128)} %param.9) | copy-start | bytes 2359300
  26.3 17.9 %collective-permute-start.2 = (f32[1024,192]{0,1:T(8,128)S(1)}, f32[1024,192]{0,1:T(8,128)S(1)}, u32[]{:S(2)}, u32[]{:S(2)}) collective-permute-start(f32[1024,192]{0,1:T(8,128)S(1)} %fusion.8), channel_id=1, source_target_pairs={{0,8},{8,0},{16,24},{24,16},{32,40},{40,32},{48,56},{56,48},{64,72... | collective-permute-start | bytes 2359304 | tf_op jit(solution)/shard_map/ppermute | solution.py:28
  44.2 23.6 %copy-start.9 = (f32[1024,192]{0,1:T(8,128)}, f32[1024,192]{0,1:T(8,128)S(1)}, u32[]{:S(2)}) copy-start(f32[1024,192]{0,1:T(8,128)S(1)} %collective-permute-done.2) | copy-start | bytes 2359300
  44.4 21.2 %collective-permute-start.3 = (f32[1024,192]{0,1:T(8,128)S(1)}, f32[1024,192]{0,1:T(8,128)S(1)}, u32[]{:S(2)}, u32[]{:S(2)}) collective-permute-start(f32[1024,192]{0,1:T(8,128)S(1)} %multiply_add_fusion.9), channel_id=1, source_target_pairs={{0,16},{8,24},{16,0},{24,8},{32,48},{40,56},{48,32},{56,40},{64,80... | collective-permute-start | bytes 2359304 | tf_op jit(solution)/shard_map/ppermute | solution.py:28
  65.6 5.4 %copy-start.11 = (f32[1024,192]{0,1:T(8,128)}, f32[1024,192]{0,1:T(8,128)S(1)}, u32[]{:S(2)}) copy-start(f32[1024,192]{0,1:T(8,128)S(1)} %collective-permute-done.3) | copy-start | bytes 2359300
  65.8 125.2 %copy-start.7 = (f32[1024,192]{0,1:T(8,128)}, f32[1024,192]{0,1:T(8,128)S(1)}, u32[]{:S(2)}) copy-start(f32[1024,192]{0,1:T(8,128)S(1)} %multiply_add_fusion.8) | copy-start | bytes 2359300
  65.8 21.1 %collective-permute-start.4 = (f32[1024,192]{0,1:T(8,128)S(1)}, f32[1024,192]{0,1:T(8,128)S(1)}, u32[]{:S(2)}, u32[]{:S(2)}) collective-permute-start(f32[1024,192]{0,1:T(8,128)S(1)} %multiply_add_fusion.8), channel_id=1, source_target_pairs={{0,32},{8,40},{16,48},{24,56},{32,0},{40,8},{48,16},{56,24},{64,96... | collective-permute-start | bytes 2359304 | tf_op jit(solution)/shard_map/ppermute | solution.py:28
  71.0 120.0 %copy-start.3 = (f32[1024,192]{0,1:T(8,128)}, f32[1024,192]{0,1:T(8,128)S(1)}, u32[]{:S(2)}) copy-start(f32[1024,192]{0,1:T(8,128)S(1)} %get-tuple-element.58) | copy-start | bytes 2359300
  71.1 40.3 %collective-permute-start.7 = (f32[1024,192]{0,1:T(8,128)S(1)}, f32[1024,192]{0,1:T(8,128)S(1)}, u32[]{:S(2)}, u32[]{:S(2)}) collective-permute-start(f32[1024,192]{0,1:T(8,128)S(1)} %get-tuple-element.57), channel_id=1, source_target_pairs={{0,128},{8,136},{16,144},{24,152},{32,160},{40,168},{48,176},{56,1... | collective-permute-start | bytes 2359304 | tf_op jit(solution)/shard_map/ppermute | solution.py:28
  86.9 104.1 %copy-start.13 = (f32[1024,192]{0,1:T(8,128)}, f32[1024,192]{0,1:T(8,128)S(1)}, u32[]{:S(2)}) copy-start(f32[1024,192]{0,1:T(8,128)S(1)} %collective-permute-done.4) | copy-start | bytes 2359300
  87.1 66.6 %collective-permute-start.5 = (f32[1024,192]{0,1:T(8,128)S(1)}, f32[1024,192]{0,1:T(8,128)S(1)}, u32[]{:S(2)}, u32[]{:S(2)}) collective-permute-start(f32[1024,192]{0,1:T(8,128)S(1)} %multiply_add_fusion.7), channel_id=1, source_target_pairs={{0,64},{8,72},{16,80},{24,88},{32,96},{40,104},{48,112},{56,120},{... | collective-permute-start | bytes 2359304 | tf_op jit(solution)/shard_map/ppermute | solution.py:28
  154.9 36.1 %collective-permute-start.6 = (f32[1024,192]{0,1:T(8,128)S(1)}, f32[1024,192]{0,1:T(8,128)}, u32[]{:S(2)}, u32[]{:S(2)}) collective-permute-start(f32[1024,192]{0,1:T(8,128)S(1)} %get-tuple-element.36), channel_id=1, source_target_pairs={{0,128},{8,136},{16,144},{24,152},{32,160},{40,168},{48,176},{56,1... | collective-permute-start | bytes 2359304 | tf_op jit(solution)/shard_map/ppermute | solution.py:28
  198.3 201.8 %reduce-scatter.3.cloned.1.call-start = ((), (), s32[]{:S(2)}) async-start(), calls=%async_computation.2 | async-start | bytes 4718592 | tf_op jit(solution)/shard_map/reduce_scatter | solution.py:106
  198.4 56.5 %copy-start.12 = (f32[1024,192]{0,1:T(8,128)S(1)}, f32[1024,192]{0,1:T(8,128)}, u32[]{:S(2)}) copy-start(f32[1024,192]{0,1:T(8,128)} %copy-done.11) | copy-start | bytes 2359300
  199.7 35.8 %collective-permute-start.8 = (f32[1024,192]{0,1:T(8,128)S(1)}, f32[1024,192]{0,1:T(8,128)S(1)}, u32[]{:S(2)}, u32[]{:S(2)}) collective-permute-start(f32[1024,192]{0,1:T(8,128)S(1)} %broadcast_multiply_fusion.1), channel_id=1, source_target_pairs={{0,64},{8,72},{16,80},{24,88},{32,96},{40,104},{48,112},{56,120},{... | collective-permute-start | bytes 2359304 | tf_op jit(solution)/shard_map/ppermute | solution.py:28
  237.5 35.7 %copy-start.10 = (f32[1024,192]{0,1:T(8,128)S(1)}, f32[1024,192]{0,1:T(8,128)}, u32[]{:S(2)}) copy-start(f32[1024,192]{0,1:T(8,128)} %copy-done.9) | copy-start | bytes 2359300
  237.7 17.2 %collective-permute-start.9 = (f32[1024,192]{0,1:T(8,128)S(1)}, f32[1024,192]{0,1:T(8,128)S(1)}, u32[]{:S(2)}, u32[]{:S(2)}) collective-permute-start(f32[1024,192]{0,1:T(8,128)S(1)} %broadcast_multiply_fusion.2), channel_id=1, source_target_pairs={{0,32},{8,40},{16,48},{24,56},{32,0},{40,8},{48,16},{56,24},{64,96... | collective-permute-start | bytes 2359304 | tf_op jit(solution)/shard_map/ppermute | solution.py:28
  255.4 17.8 %collective-permute-start.10 = (f32[1024,192]{0,1:T(8,128)S(1)}, f32[1024,192]{0,1:T(8,128)S(1)}, u32[]{:S(2)}, u32[]{:S(2)}) collective-permute-start(f32[1024,192]{0,1:T(8,128)S(1)} %broadcast_multiply_fusion.3), channel_id=1, source_target_pairs={{0,16},{8,24},{16,0},{24,8},{32,48},{40,56},{48,32},{56,40},{64,80... | collective-permute-start | bytes 2359304 | tf_op jit(solution)/shard_map/ppermute | solution.py:28
  273.7 22.6 %copy-start.4 = (f32[1024,192]{0,1:T(8,128)S(1)}, f32[1024,192]{0,1:T(8,128)}, u32[]{:S(2)}) copy-start(f32[1024,192]{0,1:T(8,128)} %copy-done.3) | copy-start | bytes 2359300
  273.7 15.4 %collective-permute-start.11 = (f32[1024,192]{0,1:T(8,128)S(1)}, f32[1024,192]{0,1:T(8,128)S(1)}, u32[]{:S(2)}, u32[]{:S(2)}) collective-permute-start(f32[1024,192]{0,1:T(8,128)S(1)} %broadcast_multiply_fusion.4), channel_id=1, source_target_pairs={{0,8},{8,0},{16,24},{24,16},{32,40},{40,32},{48,56},{56,48},{64,72... | collective-permute-start | bytes 2359304 | tf_op jit(solution)/shard_map/ppermute | solution.py:28
  289.0 0.9 copy-start.14
  296.2 7.4 %copy-start.2 = (f32[1,1024,1024]{2,1,0:T(8,128)S(1)}, f32[1,1024,1024]{2,1,0:T(8,128)}, u32[]{:S(2)}) copy-start(f32[1,1024,1024]{2,1,0:T(8,128)} %param.13) | copy-start | bytes 12582916
  296.2 7.4 %copy-start.6 = (f32[1024,192]{0,1:T(8,128)S(1)}, f32[1024,192]{0,1:T(8,128)}, u32[]{:S(2)}) copy-start(f32[1024,192]{0,1:T(8,128)} %param.9) | copy-start | bytes 2359300
  303.7 7.0 %copy-start.8 = (f32[1024,192]{0,1:T(8,128)}, f32[1024,192]{0,1:T(8,128)S(1)}, u32[]{:S(2)}) copy-start(f32[1024,192]{0,1:T(8,128)S(1)} %fusion.11) | copy-start | bytes 2359300
  310.8 83.7 %collective-permute-start.12 = (f32[2,1,192]{1,2,0:T(8,128)S(1)}, f32[2,1,192]{1,2,0:T(8,128)S(1)}, u32[]{:S(2)}, u32[]{:S(2)}) collective-permute-start(f32[2,1,192]{1,2,0:T(8,128)S(1)} %get-tuple-element.34), channel_id=1, source_target_pairs={{8,0},{16,8},{24,16},{32,24},{40,32},{48,40},{56,48},{64,56},{72,6... | collective-permute-start | bytes 4616 | tf_op jit(solution)/shard_map/ppermute | solution.py:22
  312.1 82.4 %collective-permute-start.13 = (f32[2,1,192]{1,2,0:T(8,128)S(1)}, f32[2,1,192]{1,2,0:T(8,128)S(1)}, u32[]{:S(2)}, u32[]{:S(2)}) collective-permute-start(f32[2,1,192]{1,2,0:T(8,128)S(1)} %get-tuple-element.35), channel_id=1, source_target_pairs={{0,8},{8,16},{16,24},{24,32},{32,40},{40,48},{48,56},{56,64},{64,7... | collective-permute-start | bytes 4616 | tf_op jit(solution)/shard_map/ppermute | solution.py:19
Sparse Core Ops, SparseCore 0:
  198.5 33.6 reduce-scatter.4
  296.3 38.8 reduce-scatter.2
where the time goes:
time: 409 us
  waiting for transfers between devices  212 us (52%)
  blocking collectives  77.2 us (19%)
  starting transfers between devices  48.5 us (12%)
  matrix products  36.9 us (9%)
  other arithmetic  16.5 us (4%)
  between operations  14.4 us (4%)
    ppermute x10, waiting for transfers between devices, partner_2(): lax.ppermute(shard, axis, [(i, i ^ 1 << bit) for i in range(lax.axis_size...  208 us
    psum x1, blocking collectives, local(): kernel_total = lax.psum(kernel_terms, 'seq')  77.2 us
    ppermute x10, starting transfers between devices, partner_2(): lax.ppermute(shard, axis, [(i, i ^ 1 << bit) for i in range(lax.axis_size...  37.8 us
    dot_general x2, matrix products, matmul(): jnp.dot(left, right, precision=exact_mode, preferred_element_type=jnp.flo...  15 us
    dot_general x2, matrix products, right_transposed(): lax.dot_general(left, right, (((1,), (1,)), ((), ())), precision=exact_mo...  13.6 us
    dot_general x2, matrix products, left_transposed(): lax.dot_general(left, right, (((0,), (0,)), ((), ())), precision=exact_mo...  8.34 us
  transfers between devices with their start and end apart: 16, of which 12 were waited for; matrix products, arithmetic and copies ran while one was open for 9% of the time, Pallas kernels for 0%

commit v1 on v0

v1 whole, which is shorter than its diff:
```python
import math

import jax
import jax.numpy as jnp
from jax import lax
from jax.experimental import pallas as pl
from jax.experimental.pallas import tpu as pltpu
from jax.sharding import PartitionSpec as P

D = 1536
SECTIONS = 5
BLOCKS = 32
PARTS = ((0, 4), (4, 6))
LANE_OF_PART = (0, 64)

three_pass = lax.Precision.HIGH


def contract(left, right, left_dim, right_dim):
    return lax.dot_general(
        left,
        right,
        (((left_dim,), (right_dim,)), ((), ())),
        precision=three_pass,
        preferred_element_type=jnp.float32,
    )


def to_tiles(values):
    first = values[:128].reshape(16, 8, 2, 4, 128).transpose(0, 2, 3, 1, 4).reshape(32, 4, 8, 128)
    second = values[128:].reshape(8, 8, 4, 2, 128).transpose(0, 2, 3, 1, 4).reshape(32, 2, 8, 128)
    return jnp.concatenate([first, second], axis=1)


def from_tiles(tiles):
    first = tiles[:, :4].reshape(16, 2, 4, 8, 128).transpose(0, 3, 1, 2, 4).reshape(128, 1024)
    second = tiles[:, 4:].reshape(8, 4, 2, 8, 128).transpose(0, 3, 1, 2, 4).reshape(64, 1024)
    return jnp.concatenate([first, second], axis=0)


def weights_to_tile(weights):
    first = jnp.repeat(weights[:128].reshape(16, 8, 2 * SECTIONS), 2, axis=0)
    second = jnp.repeat(weights[128:].reshape(8, 8, 2 * SECTIONS), 4, axis=0)
    gap = ((0, 0), (0, 0), (0, 64 - 2 * SECTIONS))
    return jnp.concatenate([jnp.pad(first, gap), jnp.pad(second, gap)], axis=2)[:, None]


def tile_to_weights(tile):
    first = tile[:, :, : 2 * SECTIONS].reshape(16, 2, 8, 2 * SECTIONS).sum(axis=1)
    second = tile[:, :, 64 : 64 + 2 * SECTIONS].reshape(8, 4, 8, 2 * SECTIONS).sum(axis=1)
    return jnp.concatenate([first.reshape(128, 2 * SECTIONS), second.reshape(64, 2 * SECTIONS)], axis=0)


def flip(values, section):
    stride = 2**section
    pieces = []
    for at in range(0, BLOCKS, 2 * stride):
        pieces.append(values[at + stride : at + 2 * stride])
        pieces.append(values[at : at + stride])
    return jnp.concatenate(pieces, axis=0)


def butterfly_kernel(in_ref, out_ref, weight_ref, level_ref, sum_ref):
    for part, (low, high) in enumerate(PARTS):
        lane = LANE_OF_PART[part]
        for at in range(2 * SECTIONS):
            column = in_ref[:, 12, :, lane + at : lane + at + 1]
            weight_ref[part, at] = jnp.broadcast_to(column, (BLOCKS, 8, 128))

        def one_tile(tile, first):
            level = in_ref[:, tile]
            for section in range(SECTIONS):
                level_ref[section] = level
                level = (
                    weight_ref[part, section] * level
                    + weight_ref[part, SECTIONS + section] * flip(level, section)
                )
            out_ref[:, tile] = level
            grad = in_ref[:, 6 + tile]
            for section in reversed(range(SECTIONS)):
                level = level_ref[section]
                own = grad * level
                other = grad * flip(level, section)
                if first:
                    sum_ref[part, section] = own
                    sum_ref[part, SECTIONS + section] = other
                else:
                    sum_ref[part, section] += own
                    sum_ref[part, SECTIONS + section] += other
                grad = weight_ref[part, section] * grad + flip(
                    weight_ref[part, SECTIONS + section] * grad, section
                )
            out_ref[:, 6 + tile] = grad

        one_tile(low, True)

        def body(tile, carry):
            one_tile(tile, False)
            return carry

        lax.fori_loop(low + 1, high, body, 0)

    lanes = lax.broadcasted_iota(jnp.int32, (BLOCKS, 8, 128), 2)
    result = jnp.zeros((BLOCKS, 8, 128), jnp.float32)
    for part in range(2):
        for at in range(2 * SECTIONS):
            total = jnp.sum(sum_ref[part, at], axis=2, keepdims=True)
            result = jnp.where(lanes == LANE_OF_PART[part] + at, total, result)
    out_ref[:, 12] = result


def butterfly(tiles):
    return pl.pallas_call(
        butterfly_kernel,
        out_shape=jax.ShapeDtypeStruct(tiles.shape, jnp.float32),
        in_specs=[pl.BlockSpec(memory_space=pltpu.VMEM)],
        out_specs=pl.BlockSpec(memory_space=pltpu.VMEM),
        scratch_shapes=[
            pltpu.VMEM((2, 2 * SECTIONS, BLOCKS, 8, 128), jnp.float32),
            pltpu.VMEM((SECTIONS, BLOCKS, 8, 128), jnp.float32),
            pltpu.VMEM((2, 2 * SECTIONS, BLOCKS, 8, 128), jnp.float32),
        ],
        compiler_params=pltpu.CompilerParams(vmem_limit_bytes=32 * 1024 * 1024),
        cost_estimate=pl.CostEstimate(flops=16_000_000, bytes_accessed=3_500_000, transcendentals=0),
        name="butterfly",
    )(tiles)


def neighbours(low_column, high_column):
    count = lax.axis_size("seq")
    before = lax.ppermute(low_column, "seq", [(i, i + 1) for i in range(count - 1)])
    after = lax.ppermute(high_column, "seq", [(i + 1, i) for i in range(count - 1)])
    return before, after


def local(signal, cotangent, kernel_q, kernel_k, block_first, block_second, mix_self, mix_partner):
    height, breadth = signal.shape
    blocks = lax.axis_size("seq")
    signal, cotangent = signal.T, cotangent.T
    taps_q, taps_k = kernel_q.T, kernel_k.T
    first, second = block_first[0], block_second[0]

    before, after = neighbours(signal[:, -1:], signal[:, :1])
    padded = jnp.concatenate([before, signal, after], axis=1)

    def conv(taps):
        return taps[:, 0:1] * padded[:, :-2] + taps[:, 1:2] * signal + taps[:, 2:3] * padded[:, 2:]

    query_conv = conv(taps_q)
    key_conv = conv(taps_k)
    gated_in = key_conv * signal
    grad_mixed = cotangent * query_conv
    first_out = contract(gated_in, first, 1, 1)
    grad_last = contract(grad_mixed, second, 1, 0)

    weights = jnp.concatenate([mix_self[:, 0], mix_partner[:, 0]], axis=0).T
    outgoing = jnp.concatenate([to_tiles(first_out), to_tiles(grad_last), weights_to_tile(weights)], axis=1)
    incoming = lax.all_to_all(outgoing, "seq", 0, 0, tiled=True)
    mixed = butterfly(incoming)
    returned = lax.all_to_all(mixed, "seq", 0, 0, tiled=True)
    level_last = from_tiles(returned[:, :6])
    grad_first_level = from_tiles(returned[:, 6:12])
    mix_grads = tile_to_weights(returned[:, 12]).T * (1.0 / math.sqrt(height))

    grad_blocks = jnp.stack(
        [contract(grad_first_level, gated_in, 0, 0), contract(grad_mixed, level_last, 0, 0)]
    )
    summed = lax.psum_scatter(grad_blocks, "ch", scatter_dimension=1, tiled=True) * (1.0 / math.sqrt(D))

    grad_gated = contract(grad_first_level, first, 1, 0)
    grad_key = grad_gated * signal
    mixed_out = contract(level_last, second, 1, 1)
    output = query_conv * mixed_out
    grad_query = cotangent * mixed_out

    edges = jnp.stack([grad_query, grad_key])
    edge_before, edge_after = neighbours(edges[:, :, -1:], edges[:, :, :1])
    edge_pad = jnp.concatenate([edge_before, edges, edge_after], axis=2)
    grad_signal = grad_gated * key_conv
    for at, taps in enumerate((taps_q, taps_k)):
        grad_signal = (
            grad_signal
            + taps[:, 0:1] * edge_pad[at, :, 2:]
            + taps[:, 1:2] * edges[at]
            + taps[:, 2:3] * edge_pad[at, :, :-2]
        )

    sums = jnp.stack(
        [
            jnp.sum(rows * shifted, axis=1)
            for rows in (grad_query, grad_key)
            for shifted in (padded[:, :-2], signal, padded[:, 2:])
        ]
    )
    sums = jnp.pad(sums.reshape(-1), (0, 16 * 128 - sums.size)).reshape(1, 16, 128)
    everyone = lax.all_to_all(jnp.broadcast_to(sums, (blocks, 16, 128)), "seq", 0, 0, tiled=True)
    tap_total = jnp.sum(everyone, axis=0).reshape(-1)[: 6 * breadth].reshape(2, 3, breadth)
    tap_total = tap_total * (1.0 / math.sqrt(height * blocks))

    return (
        output.T,
        grad_signal.T,
        tap_total[0],
        tap_total[1],
        summed[0][None],
        summed[1][None],
        mix_grads[:SECTIONS, None],
        mix_grads[SECTIONS:, None],
    )


def solution(mesh):
    return jax.shard_map(
        local,
        mesh=mesh,
        in_specs=(
            P("seq", "ch"),
            P("seq", "ch"),
            P(None, "ch"),
            P(None, "ch"),
            P("seq", None, None),
            P("seq", None, None),
            P(None, "seq", "ch"),
            P(None, "seq", "ch"),
        ),
        out_specs=(
            P("seq", "ch"),
            P("seq", "ch"),
            P(None, "ch"),
            P(None, "ch"),
            P("seq", "ch", None),
            P("seq", "ch", None),
            P(None, "seq", "ch"),
            P(None, "seq", "ch"),
        ),
        check_vma=False,
    )
```

time: 409 us -> 201 us (0.49)
  waiting for transfers between devices: 212 us -> 22.9 us
  starting transfers between devices: 48.5 us -> 16.5 us
  blocking collectives: 77.2 us -> 102 us
  matrix products: 36.9 us -> 21.8 us
  other arithmetic: 16.5 us -> 9.53 us
  local copies, waits for them, and re-layouts: 2.88 us -> 7.95 us
    ppermute x14 -> x4, waiting for transfers between devices: 212 us -> 2.27 us  [the longest x2 1.82 us: neighbours(): lax.ppermute(high_column, 'seq', [(i + 1, i) for i in range(count - 1)])]
    all_to_all x0 -> x2, blocking collectives: none -> 102 us  [the longest x1 55.9 us: local(): incoming = lax.all_to_all(outgoing, 'seq', 0, 0, tiled=True)]
    psum x1 -> x0, blocking collectives: 77.2 us -> none  [local(): kernel_total = lax.psum(kernel_terms, 'seq')]
    ppermute x14 -> x4, starting transfers between devices: 48.4 us -> 11.7 us  [the longest x2 9.11 us: neighbours(): lax.ppermute(low_column, 'seq', [(i, i + 1) for i in range(count - 1)])]
    reduce_scatter x2 -> x1, waiting for transfers between devices: 0.01 us -> 20.6 us  [local(): lax.psum_scatter(grad_blocks, 'ch', scatter_dimension=1, tiled=True)]
    dot_general x6, matrix products: 36.9 us -> 21.8 us  [contract(): lax.dot_general(left, right, (((left_dim,), (right_dim,)), ((), ())), pre...]
    mul x8 -> x3, other arithmetic: 6.66 us -> 1.38 us  [the longest x1 1.36 us: local(): lax.psum_scatter(grad_blocks, 'ch', scatter_dimension=1, tiled=True)]
    all_to_all x0 -> x1, starting transfers between devices: none -> 4.82 us  [local(): lax.all_to_all(jnp.broadcast_to(sums, (blocks, 16, 128)), 'seq', 0, 0, ti...]
  transfers between devices with their start and end apart: 16 -> 6, of which waited for: 12 -> 3; matrix products, arithmetic and copies ran while one was open for 9% -> 9% of each run, Pallas kernels for 0% -> 0%
where the time goes in v1:
time: 201 us; the launch traced here: 198 us
  blocking collectives  102 us (51%)
  waiting for transfers between devices  22.9 us (11%)
  matrix products  21.8 us (11%)
  starting transfers between devices  16.5 us (8%)
  between operations  14.4 us (7%)
  other arithmetic  9.53 us (5%)
  local copies, waits for them, and re-layouts  7.95 us (4%)
  Pallas kernels  3.25 us (2%)
    all_to_all x1, blocking collectives, local(): incoming = lax.all_to_all(outgoing, 'seq', 0, 0, tiled=True)  55.9 us
    all_to_all x1, blocking collectives, local(): returned = lax.all_to_all(mixed, 'seq', 0, 0, tiled=True)  46 us
    dot_general x6, matrix products, contract(): lax.dot_general(left, right, (((left_dim,), (right_dim,)), ((), ())), pre...  21.8 us
    reduce_scatter x1, waiting for transfers between devices, local(): lax.psum_scatter(grad_blocks, 'ch', scatter_dimension=1, tiled=True)  20.6 us
    ppermute x2, starting transfers between devices, neighbours(): lax.ppermute(low_column, 'seq', [(i, i + 1) for i in range(count - 1)])  9.11 us
    all_to_all x1, starting transfers between devices, local(): lax.all_to_all(jnp.broadcast_to(sums, (blocks, 16, 128)), 'seq', 0, 0, ti...  4.82 us
    another operation x1, other arithmetic, local(): jnp.stack([contract(grad_first_level, gated_in, 0, 0), contract(grad_mixe...  4.07 us
  transfers between devices with their start and end apart: 6, of which 3 were waited for; matrix products, arithmetic and copies ran while one was open for 9% of the time, Pallas kernels for 0%

profile of v1, /device:TPU:6, one launch (start us, length us, event | category | flops | bytes accessed | tf_op | source)
XLA Modules:
  0.0 198.2 jit_solution(4158246749910460093)
XLA Ops:
  7.2 0.0 reduce-scatter.2.cloned.1.call-start
  7.2 1.0 fusion.35
  8.2 1.3 collective-permute-start.1
  9.5 4.6 %collective-permute-start = (f32[192,1]{1,0:T(8,128)S(1)}, f32[192,1]{1,0:T(8,128)S(1)}, u32[]{:S(2)}, u32[]{:S(2)}) collective-permute-start(f32[192,1]{1,0:T(8,128)S(1)} %get-tuple-element.53), channel_id=1, source_target_pairs={{0,8},{8,16},{16,24},{24,32},{32,40},{40,48},{48,56},{56,64},{64,7... | collective-permute-start | bytes 2312 | tf_op jit(solution)/shard_map/ppermute | solution.py:131
  14.1 0.8 fusion.36
  14.9 0.8 fusion.37
  15.7 0.7 copy_bitcast_fusion
  16.5 0.1 copy.35
  16.5 0.0 copy-start
  16.5 0.1 copy.34
  16.7 0.0 copy-start.1
  16.7 0.0 collective-permute-done.1
  16.7 0.0 collective-permute-done
  16.7 5.2 %fusion.2 = f32[192,1024]{1,0:T(8,128)S(1)} fusion(f32[1,1024,1024]{2,1,0:T(8,128)} %param.13, f32[1024,192]{0,1:T(8,128)} %param.9, f32[192,1024]{1,0:T(8,128)} %bitcast.168, f32[192,1]{1,0:T(8,128)S(1)} %collective-permute-done, f32[192,1]{1,0:T(8,128)S(1)} %collective-permute-done.1, f32[192]{0:T(256)S(1)} %bitcast.198, f32[192]{0:T(256)S(1)} %bitcast.202, ...), kind=kOutput, calls=%fused_computation.3 | convolution fusion | flops 1209532416 | bytes 6557440 | tf_op jit(solution)/shard_map/dot_general | solution.py:20
  22.0 0.0 copy-done
  22.0 0.0 copy-done.1
  22.0 2.6 %fusion.6 = f32[192,1024]{1,0:T(8,128)S(1)} fusion(f32[1,1024,1024]{2,1,0:T(8,128)S(1)} %copy-done.1, f32[192,1024]{1,0:T(8,128)S(1)} %bitcast.169, f32[192]{0:T(256)S(1)} %bitcast.209, f32[192,1]{1,0:T(8,128)S(1)} %collective-permute-done, f32[192,1]{1,0:T(8,128)S(1)} %collective-permute-done.1, f32[192]{0:T(256)S(1)} %bitcast.212, f32[192]{0:T(256)S(1)} %bitcast.206), kind=kOutput, calls=%fused_computation.7 | convolution fusion | flops 1209532416 | bytes 5771008 | tf_op jit(solution)/shard_map/dot_general | solution.py:20
  24.8 0.1 fusion.23
  24.9 55.9 %all_to_all.15.in_ref = f32[32,13,8,128]{3,2,1,0:T(8,128)S(1)} all-to-all(f32[32,13,8,128]{3,2,1,0:T(8,128)S(1)} %fusion.23), channel_id=1, replica_groups=mesh['seq'=32,'ch'=8] {'seq'}, dimensions={0} | all-to-all | bytes 3407872 | tf_op jit(solution)/shard_map/all_to_all | solution.py:158
  80.8 0.0 copy-start.3
  80.8 3.3 %butterfly.1 = f32[32,13,8,128]{3,2,1,0:T(8,128)S(1)} custom-call(f32[32,13,8,128]{3,2,1,0:T(8,128)S(1)} %all_to_all.15.in_ref), custom_call_target="tpu_custom_call" | custom-call | flops 16000000 | bytes 3500000 | tf_op jit(solution)/shard_map/butterfly/pallas_call | solution.py:113
  84.1 46.0 %all_to_all.16 = f32[32,13,8,128]{3,2,1,0:T(8,128)S(1)} all-to-all(f32[32,13,8,128]{3,2,1,0:T(8,128)S(1)} %butterfly.1), channel_id=1, replica_groups=mesh['seq'=32,'ch'=8] {'seq'}, dimensions={0} | all-to-all | bytes 3407872 | tf_op jit(solution)/shard_map/all_to_all | solution.py:160
  130.1 0.0 copy-start.6
  130.1 0.0 copy-start.5
  130.2 0.1 fusion.32
  130.3 0.0 copy-start.4
  130.3 0.0 copy-done.3
  130.3 2.6 %convolution_bitcast_fusion = f32[1,1024,1024]{2,1,0:T(8,128)S(1)} fusion(f32[64,1024]{1,0:T(8,128)S(1)} %bitcast.182, f32[128,1024]{1,0:T(8,128)S(1)} %bitcast.176, f32[1024,192]{0,1:T(8,128)S(1)} %copy-done.3, f32[192,1024]{1,0:T(8,128)S(1)} %bitcast.170, f32[192,1]{1,0:T(8,128)S(1)} %collective-permute-done, f32[192,1]{1,0:T(8,128)S(1)} %collective-permute-done.1, ...), kind=kOutput, calls=%fused_computation.9 | convolution fusion | flops 1209729024 | bytes 6557440 | tf_op jit(solution)/shard_map/dot_general | solution.py:20
  132.9 0.0 copy-done.6
  132.9 0.0 copy-done.4
  132.9 0.0 copy-done.5
  132.9 2.5 %convolution_bitcast_fusion.1 = f32[1,1024,1024]{2,1,0:T(8,128)S(1)} fusion(f32[64,1024]{1,0:T(8,128)S(1)} %bitcast.180, f32[128,1024]{1,0:T(8,128)S(1)} %bitcast.178, f32[192,1024]{1,0:T(8,128)S(1)} %bitcast.171, f32[192]{0:T(256)S(1)} %bitcast.210, f32[192,1]{1,0:T(8,128)S(1)} %collective-permute-done, f32[192,1]{1,0:T(8,128)S(1)} %collective-permute-done.1, ...), kind=kOutput, calls=%fused_computation.10 | convolution fusion | flops 1209729024 | bytes 5771008 | tf_op jit(solution)/shard_map/dot_general | solution.py:20
  135.4 4.1 %pad_maximum_fusion = f32[2,1024,1024]{2,1,0:T(8,128)} fusion(f32[1,1024,1024]{2,1,0:T(8,128)S(1)} %convolution_bitcast_fusion, f32[1,1024,1024]{2,1,0:T(8,128)S(1)} %convolution_bitcast_fusion.1), kind=kLoop, calls=%fused_computation | loop fusion | flops 2097152 | bytes 16777216 | tf_op jit(solution)/shard_map/stack | solution.py:165
  139.5 0.0 reduce-scatter.2.cloned.1.call-update
  139.6 0.1 copy.36
  139.6 0.1 bitcast_reduce_fusion
  139.8 0.1 copy.37
  139.8 0.0 copy-start.2
  139.8 4.1 %fusion.4 = f32[192,1024]{1,0:T(8,128)S(1)} fusion(f32[1,1024,1024]{2,1,0:T(8,128)} %param.12, f32[64,1024]{1,0:T(8,128)} %bitcast.181, f32[128,1024]{1,0:T(8,128)S(1)} %bitcast.179), kind=kOutput, calls=%fused_computation.5 | convolution fusion | flops 1208156160 | bytes 5767168 | tf_op jit(solution)/shard_map/dot_general | solution.py:20
  143.9 0.0 copy-done.2
  143.9 4.8 %multiply_reduce_fusion.3 = (f32[192]{0:T(256)S(1)}, f32[192]{0:T(256)S(1)}, f32[192]{0:T(256)S(1)}, f32[192]{0:T(256)S(1)}, f32[192]{0:T(256)S(1)}, /*index=5*/...) fusion(f32[192,1]{1,0:T(8,128)S(1)} %collective-permute-done.1, ...), kind=kOutput, calls=%fused_computation.39 | convolution fusion | flops 1212480384 | bytes 10494208 | tf_op jit(solution)/shard_map/dot_general | solution.py:20
  148.8 0.1 reshape.119
  148.9 0.7 broadcast_in_dim.26
  149.6 4.8 %all-to-all-start.2 = ((f32[32,16,128]{2,1,0:T(8,128)}), f32[32,16,128]{2,1,0:T(8,128)}, u32[]{:S(2)}, u32[]{:S(2)}) async-start(f32[32,16,128]{2,1,0:T(8,128)} %broadcast_in_dim.26), calls=%async_computation.2 | async-start | bytes 524288 | tf_op jit(solution)/shard_map/all_to_all | solution.py:196
  154.4 0.1 pad_maximum_fusion.14
  154.5 1.3 collective-permute-start.2
  155.8 4.6 %collective-permute-start.3 = (f32[2,192,1]{2,1,0:T(8,128)S(1)}, f32[2,192,1]{2,1,0:T(8,128)S(1)}, u32[]{:S(2)}, u32[]{:S(2)}) collective-permute-start(f32[2,192,1]{2,1,0:T(8,128)S(1)} %get-tuple-element.48), channel_id=1, source_target_pairs={{0,8},{8,16},{16,24},{24,32},{32,40},{40,48},{48,56},{56,64},{64,7... | collective-permute-start | bytes 4616 | tf_op jit(solution)/shard_map/ppermute | solution.py:131
  160.4 0.6 copy.33
  161.0 0.6 copy.32
  161.6 1.8 collective-permute-done.2
  163.5 0.4 collective-permute-done.3
  163.9 2.7 %fusion.11 = f32[1024,192]{0,1:T(8,128)} fusion(f32[2,192,1]{2,1,0:T(8,128)S(1)} %collective-permute-done.3, f32[1,192,1024]{2,1,0:T(8,128)S(1)} %get-tuple-element.49, f32[1,192,1024]{2,1,0:T(8,128)S(1)} %bitcast.175, f32[2,192,1]{2,1,0:T(8,128)S(1)} %collective-permute-done.2, f32[192,1024]{1,0:T(8,128)S(1)} %get-tuple-element.41, ...), kind=kLoop, calls=%fused_computation.15 | loop fusion | flops 5701632 | bytes 5514240 | tf_op jit(solution)/shard_map/transpose | solution.py:202
  166.6 0.0 all-to-all-done.2
  166.6 1.0 reduce_sum.87
  167.6 0.1 mul.194
  167.7 0.6 slice_bitcast_fusion.3
  168.3 20.6 %reduce-scatter.2.cloned.1.call-done = f32[2,128,1024]{2,1,0:T(8,128)} async-done(((f32[2,1024,1024]{2,1,0:T(8,128)}), f32[2,128,1024]{2,1,0:T(8,128)}) %reduce-scatter.2.cloned.1.call-update) | async-done | bytes 1048592 | tf_op jit(solution)/shard_map/reduce_scatter | solution.py:168
  188.9 1.4 broadcast_multiply_fusion
  190.3 1.1 fusion.34
  (21 shorter events, 0.4 us)
Async XLA Ops:
  7.2 181.7 %reduce-scatter.2.cloned.1.call-start = ((), (), s32[]{:S(2)}) async-start(), calls=%async_computation.4 | async-start | bytes 9437184 | tf_op jit(solution)/shard_map/reduce_scatter | solution.py:168
  8.2 8.4 %collective-permute-start.1 = (f32[192,1]{1,0:T(8,128)S(1)}, f32[192,1]{1,0:T(8,128)S(1)}, u32[]{:S(2)}, u32[]{:S(2)}) collective-permute-start(f32[192,1]{1,0:T(8,128)S(1)} %get-tuple-element.52), channel_id=1, source_target_pairs={{8,0},{16,8},{24,16},{32,24},{40,32},{48,40},{56,48},{64,56},{72,6... | collective-permute-start | bytes 2312 | tf_op jit(solution)/shard_map/ppermute | solution.py:132
  9.5 7.1 %collective-permute-start = (f32[192,1]{1,0:T(8,128)S(1)}, f32[192,1]{1,0:T(8,128)S(1)}, u32[]{:S(2)}, u32[]{:S(2)}) collective-permute-start(f32[192,1]{1,0:T(8,128)S(1)} %get-tuple-element.53), channel_id=1, source_target_pairs={{0,8},{8,16},{16,24},{24,32},{32,40},{40,48},{48,56},{56,64},{64,7... | collective-permute-start | bytes 2312 | tf_op jit(solution)/shard_map/ppermute | solution.py:131
  16.5 5.4 %copy-start = (f32[1024,192]{0,1:T(8,128)S(1)}, f32[1024,192]{0,1:T(8,128)}, u32[]{:S(2)}) copy-start(f32[1024,192]{0,1:T(8,128)} %param.8) | copy-start | bytes 2359300
  16.7 5.3 %copy-start.1 = (f32[1,1024,1024]{2,1,0:T(8,128)S(1)}, f32[1,1024,1024]{2,1,0:T(8,128)}, u32[]{:S(2)}) copy-start(f32[1,1024,1024]{2,1,0:T(8,128)} %param.12) | copy-start | bytes 12582916
  80.8 49.5 %copy-start.3 = (f32[1024,192]{0,1:T(8,128)S(1)}, f32[1024,192]{0,1:T(8,128)}, u32[]{:S(2)}) copy-start(f32[1024,192]{0,1:T(8,128)} %param.9) | copy-start | bytes 2359300
  130.1 2.8 %copy-start.6 = (f32[32,2,8,128]{3,2,1,0:T(8,128)}, f32[32,2,8,128]{3,2,1,0:T(8,128)S(1)}, u32[]{:S(2)}) copy-start(f32[32,2,8,128]{3,2,1,0:T(8,128)S(1)} %get-tuple-element.46) | copy-start | bytes 786436
  130.1 2.8 %copy-start.5 = (f32[32,2,8,128]{3,2,1,0:T(8,128)}, f32[32,2,8,128]{3,2,1,0:T(8,128)S(1)}, u32[]{:S(2)}) copy-start(f32[32,2,8,128]{3,2,1,0:T(8,128)S(1)} %get-tuple-element.45) | copy-start | bytes 786436
  130.3 2.6 %copy-start.4 = (f32[32,4,8,128]{3,2,1,0:T(8,128)}, f32[32,4,8,128]{3,2,1,0:T(8,128)S(1)}, u32[]{:S(2)}) copy-start(f32[32,4,8,128]{3,2,1,0:T(8,128)S(1)} %get-tuple-element.44) | copy-start | bytes 1572868
  139.8 4.1 %copy-start.2 = (f32[1,1024,1024]{2,1,0:T(8,128)S(1)}, f32[1,1024,1024]{2,1,0:T(8,128)}, u32[]{:S(2)}) copy-start(f32[1,1024,1024]{2,1,0:T(8,128)} %param.13) | copy-start | bytes 12582916
  149.6 17.0 %all-to-all-start.2 = ((f32[32,16,128]{2,1,0:T(8,128)}), f32[32,16,128]{2,1,0:T(8,128)}, u32[]{:S(2)}, u32[]{:S(2)}) async-start(f32[32,16,128]{2,1,0:T(8,128)} %broadcast_in_dim.26), calls=%async_computation.2 | async-start | bytes 524288 | tf_op jit(solution)/shard_map/all_to_all | solution.py:196
  154.5 8.9 %collective-permute-start.2 = (f32[2,192,1]{2,1,0:T(8,128)S(1)}, f32[2,192,1]{2,1,0:T(8,128)S(1)}, u32[]{:S(2)}, u32[]{:S(2)}) collective-permute-start(f32[2,192,1]{2,1,0:T(8,128)S(1)} %get-tuple-element.47), channel_id=1, source_target_pairs={{8,0},{16,8},{24,16},{32,24},{40,32},{48,40},{56,48},{64,56},{72,6... | collective-permute-start | bytes 4616 | tf_op jit(solution)/shard_map/ppermute | solution.py:132
  155.8 8.1 %collective-permute-start.3 = (f32[2,192,1]{2,1,0:T(8,128)S(1)}, f32[2,192,1]{2,1,0:T(8,128)S(1)}, u32[]{:S(2)}, u32[]{:S(2)}) collective-permute-start(f32[2,192,1]{2,1,0:T(8,128)S(1)} %get-tuple-element.48), channel_id=1, source_target_pairs={{0,8},{8,16},{16,24},{24,32},{32,40},{40,48},{48,56},{56,64},{64,7... | collective-permute-start | bytes 4616 | tf_op jit(solution)/shard_map/ppermute | solution.py:131
Sparse Core Ops, SparseCore 0:
  139.7 49.1 reduce-scatter.1
